TPU v7x, 512 devices: a whole 4x4x16 slice. The times are simulated.
512 devices in a mesh: frame: 64 (over z, x_lo, core), row: 8 (over y, x_hi).
Axes of the slice: x: 4 (x_hi: 2, x_lo: 2; x = x_hi * 2 + x_lo), y: 4, z: 16, core: 2. Of those that a mesh axis runs over, the one named last changes fastest.
Arguments:
- video: bfloat16 [64, 32, 32, 3072], P('frame', 'row'), may hold values from -18 to 18
- qkv_weight: bfloat16 [3072, 3, 2048], P('frame', None, 'row'), may hold values from -1 to 1
- window: int32 [16, 3], P('row'), may hold values from 0 to 1, as said below
- clips: int32 [64], replicated, may hold values from 0 to 15, never falling along the last dimension, each value on 1 to 8 neighbouring positions
Outputs:
- attended: bfloat16 [64, 32, 32, 2048], P('frame', None, None, 'row')
Inputs may be any that keep to these rules, and one draw needn't show every extreme that they name: window[h, 0], window[h, 1] and window[h, 2] are head h's reaches along frames, row tiles and column tiles; in every group of 2 consecutive heads along each of the three, some head has reach 1. `clips`: clip numbers never fall along the frames; each clip has 1 to 8 frames.
All inputs are finite; a program needn't handle non-finite values.
Results may differ from a plain program's by a relative error of at most 0.0068.
Values may be sent and summed in bfloat16 or wider, within the bound.
No kernel may reach another device: no remote copies, remote signals or barrier semaphores. Data moves between devices by JAX's collectives and lax.ppermute only.
A program may use at most 64 MiB of HBM per device.

v0:
```python
import math
import jax
import jax.numpy as jnp
from jax import lax
from jax.sharding import PartitionSpec as P

HD = 128
TH = 8
TW = 8


def with_halo(value, sides, width):
    for axis, dim in sides:
        count, length = (lax.axis_size(axis), value.shape[dim])
        up = [(i, (i + 1) % count) for i in range(count - 1)]
        down = [(j, i) for i, j in up]
        last = lax.slice_in_dim(value, length - width, length, axis=dim)
        initial = lax.slice_in_dim(value, 0, width, axis=dim)
        before = lax.ppermute(last, axis, up)
        after = lax.ppermute(initial, axis, down)
        value = jnp.concatenate([before, value, after], axis=dim)
    return value


def body(video, qkv_weight, window, clips):
    frame_here = lax.axis_index("frame")
    local_width = qkv_weight.shape[2]
    head_count = local_width // HD
    features = video.shape[3]
    qkv_matrix = lax.all_gather(qkv_weight, "frame", axis=0, tiled=True).reshape(
        features, 3 * local_width
    )
    shard_rows = lax.all_gather(video, "row", axis=1, tiled=True)
    flattened = shard_rows.reshape(-1, features)
    result = jnp.dot(flattened, qkv_matrix, preferred_element_type=jnp.float32).astype(jnp.bfloat16)
    projected = result.reshape(
        shard_rows.shape[0], shard_rows.shape[1], shard_rows.shape[2], 3 * local_width
    )
    row_count = projected.shape[1]
    col_count = projected.shape[2]
    tokens = row_count * col_count
    projected = projected.reshape(tokens, 3 * local_width)
    queries = projected[:, :local_width]
    keyval = projected[:, local_width:].reshape(1, tokens, 2 * local_width)
    nearby = with_halo(keyval, (("frame", 0),), 1)
    edge_clip = jnp.full((1,), -1, jnp.int32)
    padded_clips = jnp.concatenate([edge_clip, clips, edge_clip])
    nearby_clips = lax.dynamic_slice_in_dim(padded_clips, frame_here, 3, 0)
    same_clip = nearby_clips == nearby_clips[1]
    frame_gap = jnp.abs(jnp.arange(3) - 1)
    frame_allowed = (frame_gap[None, :] <= window[:, 0:1]) & same_clip[None, :]
    tile_count = row_count // TH
    block_tiles = tile_count
    while block_tiles % 2 == 0 and block_tiles * TH * col_count > 512:
        block_tiles = block_tiles // 2
    band_tiles = min(tile_count, block_tiles + 2)
    positions = jnp.arange(tokens)
    tile_row = positions // col_count // TH
    tile_column = positions % col_count // TW
    score_scale = 1.0 / math.sqrt(HD)
    outputs = []
    for block_index in range(tile_count // block_tiles):
        first_tile = block_index * block_tiles
        band_start = min(max(first_tile - 1, 0), tile_count - band_tiles)
        query_from = first_tile * TH * col_count
        query_count = block_tiles * TH * col_count
        key_from = band_start * TH * col_count
        key_count = band_tiles * TH * col_count
        row_gap = jnp.abs(
            tile_row[query_from : query_from + query_count, None]
            - tile_row[None, key_from : key_from + key_count]
        )
        column_gap = jnp.abs(
            tile_column[query_from : query_from + query_count, None]
            - tile_column[None, key_from : key_from + key_count]
        )
        head_blocks = []
        for head_index in range(head_count):
            low = head_index * HD
            query_head = queries[query_from : query_from + query_count, low : low + HD]
            key_head = nearby[:, :, low : low + HD].reshape(3 * key_count, HD)
            value_head = nearby[:, :, local_width + low : local_width + low + HD].reshape(
                3 * key_count, HD
            )
            scores = (
                lax.dot_general(
                    query_head,
                    key_head,
                    (((1,), (1,)), ((), ())),
                    preferred_element_type=jnp.float32,
                )
                * score_scale
            )
            inside = (row_gap <= window[head_index, 1]) & (column_gap <= window[head_index, 2])
            allowed = (frame_allowed[head_index][None, :, None] & inside[:, None, :]).reshape(
                query_count, 3 * key_count
            )
            masked = jnp.where(allowed, scores, -1e30)
            row_max = jnp.max(masked, axis=1, keepdims=True)
            weight = jnp.exp(masked - row_max)
            totals = jnp.sum(weight, axis=1, keepdims=True)
            blended = (
                jnp.dot(weight.astype(jnp.bfloat16), value_head, preferred_element_type=jnp.float32)
                / totals
            )
            head_blocks.append(blended.astype(jnp.bfloat16))
        outputs.append(jnp.concatenate(head_blocks, axis=1))
    attended = jnp.concatenate(outputs, axis=0)
    return attended.reshape(1, row_count, col_count, local_width)


def solution(mesh):
    placed = (P("frame", "row", None, None), P("frame", None, "row"), P("row", None), P())
    return jax.shard_map(
        body, mesh=mesh, in_specs=placed, out_specs=P("frame", None, None, "row"), check_vma=False
    )
```

profile of v0, /device:TPU:98, one launch (start us, length us, event | category | flops | bytes accessed | tf_op | source)
XLA Modules:
  0.0 308.2 jit_solution(17706026127067027402)
XLA Ops:
  6.5 0.7 all-gather.5.cloned.1.call-update
  8.0 1.5 fusion.80
  9.5 128.0 %all-gather.5.cloned.1.call-done = bf16[3072,3,256]{2,0,1:T(8,128)(2,1)} async-done(((bf16[48,3,256]{2,0,1:T(8,128)(2,1)}), bf16[3072,3,256]{2,0,1:T(8,128)(2,1)}) %all-gather.5.cloned.1.call-update) | async-done | bytes 4718608 | tf_op jit(solution)/shard_map/all_gather | solution.py:30
  137.5 6.7 %copy.14 = bf16[3072,3,256]{0,2,1:T(8,128)(2,1)} copy(bf16[3072,3,256]{2,0,1:T(8,128)(2,1)} %all-gather.5.cloned.1.call-done) | data formatting | bytes 9437184 | tf_op jit(solution)/shard_map/all_gather | solution.py:30
  144.1 97.2 %all-gather.3.cloned.1.call-done = bf16[1,32,32,3072]{3,2,0,1:T(8,128)(2,1)} async-done(((bf16[1,4,32,3072]{3,2,0,1:T(8,128)(2,1)}), bf16[1,32,32,3072]{3,2,0,1:T(8,128)(2,1)}) %all-gather.3.cloned.1.call-update) | async-done | bytes 6291472 | tf_op jit(solution)/shard_map/all_gather | solution.py:33
  241.3 8.6 %convolution_convert_fusion = bf16[1024,768]{1,0:T(8,128)(2,1)S(1)} fusion(bf16[1024,3072]{1,0:T(8,128)(2,1)} %bitcast.47, bf16[3072,768]{0,1:T(8,128)(2,1)} %bitcast.45), kind=kOutput, calls=%fused_computation.41 | convolution fusion | flops 4832624640 | bytes 12582912 | tf_op jit(solution)/shard_map/dot_general | solution.py:35
  249.9 1.1 slice_bitcast_fusion
  251.0 2.4 collective-permute-start.1
  253.4 1.9 collective-permute-start
  255.4 6.5 %fusion.28 = (pred[512,1024]{0,1:T(8,128)(4,1)}, pred[512,1024]{0,1:T(8,128)(4,1)}, pred[512,1024]{0,1:T(8,128)(4,1)S(1)}, pred[512,1024]{0,1:T(8,128)(4,1)S(1)}) fusion(s32[]{:T(128)} %bitcast.3, s32[1024]{0:T(1024)S(1)} %get-tuple-element.33, s32[512]{0:T(512)S(1)} %get-tuple-element.17, s32[]{:T(128)} %bitcast.2, s32[1024]{0:T(1024)S(1)} %get-tuple-element.34, ...), kind=kLoop, calls=%fused_computation.37 | loop fusion | flops 10485760 | bytes 2113552 | tf_op jit(solution)/shard_map/and | solution.py:94
  262.3 1.7 copy.17
  266.2 1.7 copy.16
  268.0 1.5 and.202
  269.6 1.7 copy.15
  271.7 1.7 copy.12
  273.4 3.9 %collective-permute-done.1 = bf16[1,1024,512]{2,1,0:T(8,128)(2,1)} collective-permute-done((bf16[1,1024,512]{2,1,0:T(8,128)(2,1)}, bf16[1,1024,512]{2,1,0:T(8,128)(2,1)}, u32[]{:S(2)}, u32[]{:S(2)}) %collective-permute-start.1) | collective-permute-done | bytes 1048608 | tf_op jit(solution)/shard_map/ppermute | solution.py:20
  277.3 3.6 %collective-permute-done = bf16[1,1024,512]{2,1,0:T(8,128)(2,1)} collective-permute-done((bf16[1,1024,512]{2,1,0:T(8,128)(2,1)}, bf16[1,1024,512]{2,1,0:T(8,128)(2,1)}, u32[]{:S(2)}, u32[]{:S(2)}) %collective-permute-start) | collective-permute-done | bytes 1048608 | tf_op jit(solution)/shard_map/ppermute | solution.py:19
  280.9 2.2 pad_maximum_fusion
  283.7 0.8 copy-done.1
  284.5 1.6 fusion.81
  286.2 1.9 fusion.83
  288.0 1.0 fusion.6
  289.0 1.3 fusion.53
  290.3 1.0 fusion.2
  291.3 1.3 fusion.41
  292.6 1.6 fusion.82
  294.2 1.6 fusion.84
  295.8 1.0 fusion.4
  296.8 1.3 fusion.47
  298.1 1.0 fusion
  299.1 1.3 fusion.35
  300.4 1.0 copy.18
  (32 shorter events, 4.5 us)
Async XLA Ops:
  6.5 130.9 %all-gather.5.cloned.1.call-start = ((), (), s32[]{:S(2)}) async-start(), calls=%async_computation.1 | async-start | bytes 4792320 | tf_op jit(solution)/shard_map/all_gather | solution.py:30
  7.3 234.1 %all-gather.3.cloned.1.call-start = ((), (), s32[]{:S(2)}) async-start(), calls=%async_computation | async-start | bytes 7077888 | tf_op jit(solution)/shard_map/all_gather | solution.py:33
  249.9 12.4 %copy-start = (bf16[1024,768]{1,0:T(8,128)(2,1)}, bf16[1024,768]{1,0:T(8,128)(2,1)S(1)}, u32[]{:S(2)}) copy-start(bf16[1024,768]{1,0:T(8,128)(2,1)S(1)} %convolution_convert_fusion) | copy-start | bytes 4718596
  251.0 26.2 %collective-permute-start.1 = (bf16[1,1024,512]{2,1,0:T(8,128)(2,1)}, bf16[1,1024,512]{2,1,0:T(8,128)(2,1)}, u32[]{:S(2)}, u32[]{:S(2)}) collective-permute-start(bf16[1,1024,512]{2,1,0:T(8,128)(2,1)} %slice_bitcast_fusion), channel_id=1, source_target_pairs={{8,0},{16,8},{24,16},{32,24},{40,32},{48,40},{56,48},{64,56},{72,6... | collective-permute-start | bytes 3145736 | tf_op jit(solution)/shard_map/ppermute | solution.py:20
  253.4 27.5 %collective-permute-start = (bf16[1,1024,512]{2,1,0:T(8,128)(2,1)}, bf16[1,1024,512]{2,1,0:T(8,128)(2,1)}, u32[]{:S(2)}, u32[]{:S(2)}) collective-permute-start(bf16[1,1024,512]{2,1,0:T(8,128)(2,1)} %slice_bitcast_fusion), channel_id=1, source_target_pairs={{0,8},{8,16},{16,24},{24,32},{32,40},{40,48},{48,56},{56,64},{64,7... | collective-permute-start | bytes 3145736 | tf_op jit(solution)/shard_map/ppermute | solution.py:19
  261.9 2.1 copy-start.4
  261.9 3.6 %copy-start.3 = (s32[2,3]{1,0:T(2,128)S(1)}, s32[2,3]{1,0:T(2,128)}, u32[]{:S(2)}) copy-start(s32[2,3]{1,0:T(2,128)} %param.6) | copy-start | bytes 76
  268.0 3.2 %copy-start.2 = (pred[512,1024]{0,1:T(8,128)(4,1)S(1)}, pred[512,1024]{0,1:T(8,128)(4,1)}, u32[]{:S(2)}) copy-start(pred[512,1024]{0,1:T(8,128)(4,1)} %get-tuple-element.9) | copy-start | bytes 1572868
  283.1 1.4 copy-start.1
Sparse Core Ops, SparseCore 0:
  9.5 127.9 all-gather.4
  140.6 100.6 all-gather.2
where the time goes:
time: 309 us; the launch traced here: 308 us
  waiting for transfers between devices  234 us (76%)
  local copies, waits for them, and re-layouts  22.2 us (7%)
  matrix products  20.4 us (7%)
  other arithmetic  13.6 us (4%)
  between operations  13.6 us (4%)
  starting transfers between devices  4.36 us (1%)
    all_gather x1, waiting for transfers between devices, body(): lax.all_gather(qkv_weight, 'frame', axis=0, tiled=True)  128 us
    all_gather x1, waiting for transfers between devices, body(): shard_rows = lax.all_gather(video, 'row', axis=1, tiled=True)  97.2 us
    and x13, local copies, waits for them, and re-layouts, body(): frame_allowed[head_index][None, :, None] & inside[:, None, :]  9.75 us
    dot_general x1, matrix products, body(): jnp.dot(flattened, qkv_matrix, preferred_element_type=jnp.float32)  8.6 us
    dot_general x4, matrix products, body(): lax.dot_general(query_head, key_head, (((1,), (1,)), ((), ())), preferred...  6.75 us
    all_gather x1, local copies, waits for them, and re-layouts, body(): lax.all_gather(qkv_weight, 'frame', axis=0, tiled=True)  6.67 us
    and x1, other arithmetic, body(): (row_gap <= window[head_index, 1]) & (column_gap <= window[head_index, 2])  6.53 us
  transfers between devices with their start and end apart: 4, of which 4 were waited for; matrix products, arithmetic and copies ran while one was open for 8% of the time, Pallas kernels for 0%

commit v1 on v0

--- a/solution.py
+++ b/solution.py
@@ -30,7 +30,10 @@
     qkv_matrix = lax.all_gather(qkv_weight, "frame", axis=0, tiled=True).reshape(
         features, 3 * local_width
     )
-    shard_rows = lax.all_gather(video, "row", axis=1, tiled=True)
+    count_2 = lax.axis_size("row")
+    shards = jnp.stack([video for _ in range(count_2)])
+    shards = lax.all_to_all(shards, "row", split_axis=0, concat_axis=0)
+    shard_rows = jnp.concatenate(shards, axis=1)
     flattened = shard_rows.reshape(-1, features)
     result = jnp.dot(flattened, qkv_matrix, preferred_element_type=jnp.float32).astype(jnp.bfloat16)
     projected = result.reshape(

time: 309 us -> 212 us (0.69)
  the two profiles are of different devices: /device:TPU:98 before, /device:TPU:6 now
where the time goes in v1:
time: 212 us
  waiting for transfers between devices  126 us (59%)
  local copies, waits for them, and re-layouts  26 us (12%)
  matrix products  20.4 us (10%)
  other arithmetic  13.7 us (6%)
  between operations  13.6 us (6%)
  starting transfers between devices  12 us (6%)
    all_gather x1, waiting for transfers between devices, body(): lax.all_gather(qkv_weight, 'frame', axis=0, tiled=True)  119 us
    and x13, local copies, waits for them, and re-layouts, body(): frame_allowed[head_index][None, :, None] & inside[:, None, :]  9.75 us
    dot_general x1, matrix products, body(): jnp.dot(flattened, qkv_matrix, preferred_element_type=jnp.float32)  8.6 us
    all_to_all x1, starting transfers between devices, body(): shards = lax.all_to_all(shards, 'row', split_axis=0, concat_axis=0)  7.56 us
    dot_general x4, matrix products, body(): lax.dot_general(query_head, key_head, (((1,), (1,)), ((), ())), preferred...  6.75 us
    all_gather x1, local copies, waits for them, and re-layouts, body(): lax.all_gather(qkv_weight, 'frame', axis=0, tiled=True)  6.66 us
    and x1, other arithmetic, body(): (row_gap <= window[head_index, 1]) & (column_gap <= window[head_index, 2])  6.58 us
    ppermute x1, waiting for transfers between devices, with_halo(): before = lax.ppermute(last, axis, up)  6.4 us
  transfers between devices with their start and end apart: 4, of which 2 were waited for; matrix products, arithmetic and copies ran while one was open for 14% of the time, Pallas kernels for 0%

profile of v1, /device:TPU:6, one launch (start us, length us, event | category | flops | bytes accessed | tf_op | source)
XLA Modules:
  0.0 211.9 jit_solution(4767446225378603112)
XLA Ops:
  6.5 0.7 all-gather.2.cloned.1.call-update
  7.3 4.6 %stack.2 = bf16[8,1,4,32,3072]{4,3,2,1,0:T(8,128)(2,1)} broadcast(bf16[4,32,3072]{2,1,0:T(8,128)(2,1)} %bitcast.46), dimensions={2,3,4} | broadcast | bytes 7077888 | tf_op jit(solution)/shard_map/stack | solution.py:34
  11.8 7.6 %all-to-all-start = ((bf16[8,1,4,32,3072]{4,3,2,1,0:T(8,128)(2,1)}), bf16[8,1,4,32,3072]{4,3,2,1,0:T(8,128)(2,1)}, u32[]{:S(2)}, u32[]{:S(2)}) async-start(bf16[8,1,4,32,3072]{4,3,2,1,0:T(8,128)(2,1)} %stack.2), calls=%async_computation | async-start | bytes 12582912 | tf_op jit(solution)/shard_map/all_to_all | solution.py:35
  20.1 119.0 %all-gather.2.cloned.1.call-done = bf16[3072,3,256]{2,0,1:T(8,128)(2,1)} async-done(((bf16[48,3,256]{2,0,1:T(8,128)(2,1)}), bf16[3072,3,256]{2,0,1:T(8,128)(2,1)}) %all-gather.2.cloned.1.call-update) | async-done | bytes 4718608 | tf_op jit(solution)/shard_map/all_gather | solution.py:30
  139.2 6.7 %copy.13 = bf16[3072,3,256]{0,2,1:T(8,128)(2,1)} copy(bf16[3072,3,256]{2,0,1:T(8,128)(2,1)} %all-gather.2.cloned.1.call-done) | data formatting | bytes 9437184 | tf_op jit(solution)/shard_map/all_gather | solution.py:30
  145.8 8.6 %convolution_convert_fusion = bf16[1024,768]{1,0:T(8,128)(2,1)S(1)} fusion(bf16[1024,3072]{1,0:T(8,128)(2,1)} %bitcast.6, bf16[3072,768]{0,1:T(8,128)(2,1)} %bitcast.45), kind=kOutput, calls=%fused_computation.41 | convolution fusion | flops 4832624640 | bytes 12582912 | tf_op jit(solution)/shard_map/dot_general | solution.py:38
  154.4 1.1 slice_bitcast_fusion
  155.6 2.5 %collective-permute-start.1 = (bf16[1,1024,512]{2,1,0:T(8,128)(2,1)}, bf16[1,1024,512]{2,1,0:T(8,128)(2,1)}, u32[]{:S(2)}, u32[]{:S(2)}) collective-permute-start(bf16[1,1024,512]{2,1,0:T(8,128)(2,1)} %slice_bitcast_fusion), channel_id=1, source_target_pairs={{8,0},{16,8},{24,16},{32,24},{40,32},{48,40},{56,48},{64,56},{72,6... | collective-permute-start | bytes 3145736 | tf_op jit(solution)/shard_map/ppermute | solution.py:20
  158.1 1.9 collective-permute-start
  160.0 6.6 %fusion.28 = (pred[512,1024]{0,1:T(8,128)(4,1)}, pred[512,1024]{0,1:T(8,128)(4,1)}, pred[512,1024]{0,1:T(8,128)(4,1)S(1)}, pred[512,1024]{0,1:T(8,128)(4,1)S(1)}) fusion(s32[]{:T(128)} %bitcast.3, s32[1024]{0:T(1024)S(1)} %get-tuple-element.33, s32[512]{0:T(512)S(1)} %get-tuple-element.17, s32[]{:T(128)} %bitcast.2, s32[1024]{0:T(1024)S(1)} %get-tuple-element.34, ...), kind=kLoop, calls=%fused_computation.37 | loop fusion | flops 10485760 | bytes 2113552 | tf_op jit(solution)/shard_map/and | solution.py:97
  167.0 1.7 copy.16
  169.5 0.7 broadcast_compare_fusion
  170.9 1.7 copy.15
  172.7 1.5 and.202
  174.2 1.7 copy.14
  176.4 1.7 copy.12
  178.1 6.4 %collective-permute-done = bf16[1,1024,512]{2,1,0:T(8,128)(2,1)} collective-permute-done((bf16[1,1024,512]{2,1,0:T(8,128)(2,1)}, bf16[1,1024,512]{2,1,0:T(8,128)(2,1)}, u32[]{:S(2)}, u32[]{:S(2)}) %collective-permute-start) | collective-permute-done | bytes 1048608 | tf_op jit(solution)/shard_map/ppermute | solution.py:19
  184.5 2.2 %pad_maximum_fusion = bf16[3,1024,512]{2,1,0:T(8,128)(2,1)S(1)} fusion(bf16[1,1024,512]{2,1,0:T(8,128)(2,1)} %collective-permute-done.1, bf16[1,1024,512]{2,1,0:T(8,128)(2,1)} %slice_bitcast_fusion, bf16[1,1024,512]{2,1,0:T(8,128)(2,1)} %collective-permute-done), kind=kLoop, calls=%fused_computation.20 | loop fusion | flops 3145728 | bytes 6291456 | tf_op jit(solution)/shard_map/concatenate | solution.py:21
  187.3 0.8 copy-done.1
  188.1 1.6 fusion.81
  189.8 1.9 fusion.83
  191.6 1.0 fusion.6
  192.6 1.3 fusion.53
  193.9 1.0 fusion.2
  194.9 1.3 fusion.41
  196.2 1.6 fusion.82
  197.8 1.6 fusion.84
  199.4 1.0 fusion.4
  200.4 1.3 fusion.47
  201.7 1.0 fusion
  202.7 1.3 fusion.35
  204.0 1.0 copy.17
  (32 shorter events, 3.8 us)
Async XLA Ops:
  6.5 132.6 %all-gather.2.cloned.1.call-start = ((), (), s32[]{:S(2)}) async-start(), calls=%async_computation.1 | async-start | bytes 4792320 | tf_op jit(solution)/shard_map/all_gather | solution.py:30
  11.8 7.6 %copy-start.3 = (s32[2,3]{1,0:T(2,128)S(1)}, s32[2,3]{1,0:T(2,128)}, u32[]{:S(2)}) copy-start(s32[2,3]{1,0:T(2,128)} %param.6) | copy-start | bytes 76
  11.8 134.0 %all-to-all-start = ((bf16[8,1,4,32,3072]{4,3,2,1,0:T(8,128)(2,1)}), bf16[8,1,4,32,3072]{4,3,2,1,0:T(8,128)(2,1)}, u32[]{:S(2)}, u32[]{:S(2)}) async-start(bf16[8,1,4,32,3072]{4,3,2,1,0:T(8,128)(2,1)} %stack.2), calls=%async_computation | async-start | bytes 12582912 | tf_op jit(solution)/shard_map/all_to_all | solution.py:35
  154.4 12.6 %copy-start = (bf16[1024,768]{1,0:T(8,128)(2,1)}, bf16[1024,768]{1,0:T(8,128)(2,1)S(1)}, u32[]{:S(2)}) copy-start(bf16[1024,768]{1,0:T(8,128)(2,1)S(1)} %convolution_convert_fusion) | copy-start | bytes 4718596
  155.6 22.6 %collective-permute-start.1 = (bf16[1,1024,512]{2,1,0:T(8,128)(2,1)}, bf16[1,1024,512]{2,1,0:T(8,128)(2,1)}, u32[]{:S(2)}, u32[]{:S(2)}) collective-permute-start(bf16[1,1024,512]{2,1,0:T(8,128)(2,1)} %slice_bitcast_fusion), channel_id=1, source_target_pairs={{8,0},{16,8},{24,16},{32,24},{40,32},{48,40},{56,48},{64,56},{72,6... | collective-permute-start | bytes 3145736 | tf_op jit(solution)/shard_map/ppermute | solution.py:20
  158.1 26.4 %collective-permute-start = (bf16[1,1024,512]{2,1,0:T(8,128)(2,1)}, bf16[1,1024,512]{2,1,0:T(8,128)(2,1)}, u32[]{:S(2)}, u32[]{:S(2)}) collective-permute-start(bf16[1,1024,512]{2,1,0:T(8,128)(2,1)} %slice_bitcast_fusion), channel_id=1, source_target_pairs={{0,8},{8,16},{16,24},{24,32},{32,40},{40,48},{48,56},{56,64},{64,7... | collective-permute-start | bytes 3145736 | tf_op jit(solution)/shard_map/ppermute | solution.py:19
  166.6 2.1 %copy-start.4 = (s32[64]{0:T(128)S(1)}, s32[64]{0:T(128)}, u32[]{:S(2)}) copy-start(s32[64]{0:T(128)} %param.7) | copy-start | bytes 772
  172.7 3.2 %copy-start.2 = (pred[512,1024]{0,1:T(8,128)(4,1)S(1)}, pred[512,1024]{0,1:T(8,128)(4,1)}, u32[]{:S(2)}) copy-start(pred[512,1024]{0,1:T(8,128)(4,1)} %get-tuple-element.9) | copy-start | bytes 1572868
  186.7 1.4 copy-start.1
Sparse Core Ops, SparseCore 0:
  9.5 129.6 all-gather.1
